TPU v7x, 512 devices: a whole 4x4x16 slice. The times are simulated.
512 devices in a mesh: replica: 64 (over x, z), head: 8 (over y, core).
Axes of the slice: x: 4, y: 4, z: 16, core: 2. Of those that a mesh axis runs over, the one named last changes fastest.
Arguments:
- states: float32 [256, 32, 128, 128], P('replica', 'head'), may hold values from -18 to 18
- partner: int32 [64], replicated, may hold values from 0 to 63, as said below
- send_ids: int32 [64, 2], replicated, may hold values from 0 to 3, as said below
- send_count: int32 [64], replicated, may hold values from 1 to 2, as said below
- prefill_slot: int32 [64], P('replica'), may hold values from 0 to 3
- prompt_len: int32 [64], P('replica'), may hold values from 128 to 512, as said below
- decode_slots: int32 [64, 4], P('replica'), may hold values from 0 to 3, each once within a row
- q_prefill: bfloat16 [32768, 4096], P('replica', 'head'), may hold values from -6 to 6
- k_prefill: bfloat16 [32768, 4096], P('replica', 'head'), may hold values from -6 to 6
- v_prefill: bfloat16 [32768, 4096], P('replica', 'head'), may hold values from -6 to 6
- q_decode: bfloat16 [2, 256, 4096], P(None, 'replica', 'head'), may hold values from -6 to 6
- k_decode: bfloat16 [2, 256, 4096], P(None, 'replica', 'head'), may hold values from -6 to 6
- v_decode: bfloat16 [2, 256, 4096], P(None, 'replica', 'head'), may hold values from -6 to 6
- slopes: float32 [32], P('head'), may hold values from 0.003 to 0.06
- w_out: bfloat16 [4096, 3072], P('head'), may hold values from -0.125 to 0.125
Outputs:
- prefill_out: bfloat16 [32768, 3072], P('replica', 'head')
- decode_out: bfloat16 [2, 256, 3072], P(None, 'replica', 'head')
Inputs may be any that keep to these rules, and one draw needn't show every extreme that they name: partner[i] = i XOR m for one number m with 1 <= m < 64, the same for every replica, so replicas form pairs. `send_ids`: each row names 2 different slots. `send_count`: some replica sends 2 requests in every draw. `prompt_len`: some replica has 512 valid tokens in every draw.
All inputs are finite; a program needn't handle non-finite values.
Results may differ from a plain program's by a relative error of at most 0.017.
Values may be sent and summed in bfloat16 or wider, within the bound.
No kernel may reach another device: no remote copies, remote signals or barrier semaphores. Data moves between devices by JAX's collectives and lax.ppermute only.
A program may use at most 64 MiB of HBM per device.

v0:
```python
from functools import partial

import jax
import jax.numpy as jnp
from jax import lax
from jax.sharding import PartitionSpec as P

DK = 128
BLK = 128


EPS = 1e-06


def from_partner(array, axis, apart):
    return lax.ppermute(array, axis, [(i, i ^ 1 << apart) for i in range(lax.axis_size(axis))])


def head_norm(inputs):
    factor = lax.rsqrt(jnp.mean(inputs * inputs, axis=-1, keepdims=True) + EPS)
    return inputs * factor


def prefill_block(memory, inputs, slopes):
    q_block, k_block, v_block, valid_count = inputs
    row_ids = jnp.arange(q_block.shape[0], dtype=jnp.int32)
    places = row_ids.astype(jnp.float32)
    is_valid = row_ids < valid_count
    filled = valid_count.astype(jnp.float32)
    distance = jnp.maximum(places[:, None] - places[None, :], 0.0)
    causal = (row_ids[:, None] >= row_ids[None, :]) & is_valid[None, :]
    damping = jnp.where(causal[None], jnp.exp(-slopes[:, None, None] * distance[None]), 0.0)
    scores = jnp.einsum("rhd,chd->hrc", q_block, k_block, preferred_element_type=jnp.float32)
    attn_weights = (scores * damping).astype(jnp.bfloat16)
    intra_part = jnp.einsum(
        "hrc,chd->rhd", attn_weights, v_block, preferred_element_type=jnp.float32
    )
    leading = jnp.exp(-slopes[None, :] * (places[:, None] + 1.0))
    carried = jnp.einsum(
        "rhd,hde->rhe", q_block.astype(jnp.float32), memory, precision=lax.Precision.HIGHEST
    )
    attended = intra_part + leading[:, :, None] * carried
    trailing = jnp.where(
        is_valid[:, None],
        jnp.exp(-slopes[None, :] * jnp.maximum(filled - 1.0 - places, 0.0)[:, None]),
        0.0,
    )
    keys_weighted = (k_block.astype(jnp.float32) * trailing[:, :, None]).astype(jnp.bfloat16)
    update = jnp.einsum("chd,che->hde", keys_weighted, v_block, preferred_element_type=jnp.float32)
    memory = jnp.exp(-slopes * filled)[:, None, None] * memory + update
    return (memory, attended)


def pair_moves(pattern_value, bit_total, payload):
    for bit_pos in range(bit_total):
        if pattern_value >> bit_pos & 1:
            payload = from_partner(payload, "replica", bit_pos)
    return payload


def on_device(
    states,
    partner,
    send_ids,
    send_count,
    prefill_slot,
    prompt_len,
    decode_slots,
    q_prefill,
    k_prefill,
    v_prefill,
    q_decode,
    k_decode,
    v_decode,
    slopes,
    w_out,
):
    own_index = lax.axis_index("replica")
    mate = partner[own_index]
    own_ids = send_ids[own_index]
    payload = jnp.take(states, own_ids, axis=0)
    pattern = jnp.bitwise_xor(mate, own_index)
    bit_total = lax.axis_size("replica").bit_length() - 1
    branches = [
        partial(pair_moves, value, bit_total) for value in range(1, lax.axis_size("replica"))
    ]
    payload = lax.switch(jnp.clip(pattern - 1, 0, lax.axis_size("replica") - 2), branches, payload)
    slot_count = states.shape[0]
    slot_ids = jnp.arange(slot_count, dtype=jnp.int32)
    mate_ids = send_ids[mate]
    own_count = send_count[own_index]
    mate_count = send_count[mate]
    leaving = jnp.zeros((slot_count,), dtype=jnp.bool_)
    for entry in range(own_ids.shape[0]):
        leaving = leaving | (slot_ids == own_ids[entry]) & (entry < own_count)
    moved = jnp.where(leaving[:, None, None, None], jnp.float32(0.0), states)
    for entry in range(own_ids.shape[0]):
        landing = (slot_ids == mate_ids[entry]) & (entry < mate_count)
        moved = jnp.where(landing[:, None, None, None], payload[entry][None], moved)
    head_count = slopes.shape[0]
    tokens = q_prefill.shape[0]
    blocks = tokens // BLK
    length = prompt_len[0]
    start_state = lax.dynamic_index_in_dim(moved, prefill_slot[0], 0, keepdims=False)
    counts = jnp.clip(length - jnp.arange(blocks, dtype=jnp.int32) * BLK, 0, BLK)

    def shaped(source):
        return source.reshape(blocks, BLK, head_count, DK)

    final_state, attended = lax.scan(
        partial(prefill_block, slopes=slopes),
        start_state,
        (shaped(q_prefill), shaped(k_prefill), shaped(v_prefill), counts),
    )
    attended = attended.reshape(tokens, head_count, DK)
    token_ids = jnp.arange(tokens, dtype=jnp.int32)
    prefill_normed = jnp.where((token_ids < length)[:, None, None], head_norm(attended), 0.0)
    prefill_normed = prefill_normed.astype(jnp.bfloat16).reshape(tokens, head_count * DK)
    prefill_term = jnp.dot(prefill_normed, w_out, preferred_element_type=jnp.float32)
    prefill_out = lax.psum_scatter(
        prefill_term.astype(jnp.bfloat16), "head", scatter_dimension=1, tiled=True
    )
    served = lax.dynamic_update_index_in_dim(moved, final_state, prefill_slot[0], 0)
    memory = jnp.take(served, decode_slots[0], axis=0)
    keep_rate = jnp.exp(-slopes)[None, :, None, None]
    decode_rows = q_decode.shape[1]
    decode_normed = []
    for step_index in range(q_decode.shape[0]):
        keys = k_decode[step_index].reshape(decode_rows, head_count, DK)
        values_now = v_decode[step_index].reshape(decode_rows, head_count, DK)
        query = q_decode[step_index].reshape(decode_rows, head_count, DK)
        memory = keep_rate * memory + jnp.einsum(
            "rhd,rhe->rhde", keys, values_now, preferred_element_type=jnp.float32
        )
        output = jnp.einsum(
            "rhd,rhde->rhe", query.astype(jnp.float32), memory, precision=lax.Precision.HIGHEST
        )
        decode_normed.append(
            head_norm(output).astype(jnp.bfloat16).reshape(decode_rows, head_count * DK)
        )
    decode_parts = [
        lax.psum_scatter(
            jnp.dot(normed, w_out, preferred_element_type=jnp.float32).astype(jnp.bfloat16),
            "head",
            scatter_dimension=1,
            tiled=True,
        )
        for normed in decode_normed
    ]
    decode_out = jnp.stack(decode_parts)
    return (prefill_out, decode_out)


def solution(mesh):
    return jax.shard_map(
        on_device,
        mesh=mesh,
        in_specs=(
            P("replica", "head", None, None),
            P(),
            P(),
            P(),
            P("replica"),
            P("replica"),
            P("replica", None),
            P("replica", "head"),
            P("replica", "head"),
            P("replica", "head"),
            P(None, "replica", "head"),
            P(None, "replica", "head"),
            P(None, "replica", "head"),
            P("head"),
            P("head", None),
        ),
        out_specs=(P("replica", "head"), P(None, "replica", "head")),
        check_vma=False,
    )
```

profile of v0, /device:TPU:1, one launch (start us, length us, event | category | flops | bytes accessed | tf_op | source)
XLA Modules:
  0.0 347.1 jit_solution(6946031912800821939)
XLA Ops:
  7.2 1.4 dynamic_slice.49
  13.1 1.3 fusion.52
  19.8 1.2 negate_exponential_fusion
  21.6 1.3 fusion.49
  27.4 2.6 gather_fusion
  31.2 98.2 %conditional.1 = (f32[2,4,128,128]{3,2,1,0:T(8,128)}) conditional(s32[]{:T(128)} %clamp.4, f32[2,4,128,128]{3,2,1,0:T(8,128)S(1)} %broadcast_select_fusion, f32[2,4,128,128]{3,2,1,0:T(8,128)S(1)} %broadcast_select_fusion, f32[2,4,128,128]{3,2,1,0:T(8,128)S(1)} %broadcast_select_fusion, ...), branch_computations={%region_0.1_spmd, %region_1.2_spmd, %region_2.3_spmd, %region_3.4_... | conditional | bytes 12583160 | solution.py:87
  31.4 4.4 %collective-permute-start.143 = (f32[2,4,128,128]{3,2,1,0:T(8,128)S(1)}, f32[2,4,128,128]{3,2,1,0:T(8,128)S(1)}, u32[]{:S(2)}, u32[]{:S(2)}) collective-permute-start(f32[2,4,128,128]{3,2,1,0:T(8,128)S(1)} %param.52), channel_id=1, source_target_pairs={{0,8},{8,0},{16,24},{24,16},{32,40},{40,32},{48,56},{56,48},{64,72... | collective-permute-start | bytes 1572872 | tf_op jit(solution)/shard_map/cond/branch_52_fun/ppermute | solution.py:16
  35.8 7.0 %collective-permute-done.143 = f32[2,4,128,128]{3,2,1,0:T(8,128)S(1)} collective-permute-done((f32[2,4,128,128]{3,2,1,0:T(8,128)S(1)}, f32[2,4,128,128]{3,2,1,0:T(8,128)S(1)}, u32[]{:S(2)}, u32[]{:S(2)}) %collective-permute-start.143) | collective-permute-done | bytes 524320 | tf_op jit(solution)/shard_map/cond/branch_52_fun/ppermute | solution.py:16
  42.8 13.3 %collective-permute-start.144 = (f32[2,4,128,128]{3,2,1,0:T(8,128)S(1)}, f32[2,4,128,128]{3,2,1,0:T(8,128)S(1)}, u32[]{:S(2)}, u32[]{:S(2)}) collective-permute-start(f32[2,4,128,128]{3,2,1,0:T(8,128)S(1)} %collective-permute-done.143), channel_id=1, source_target_pairs={{0,32},{8,40},{16,48},{24,56},{32,0},{40,8},{48,16},{56,24},{64,96... | collective-permute-start | bytes 1572872 | tf_op jit(solution)/shard_map/cond/branch_52_fun/ppermute | solution.py:16
  56.1 45.0 %collective-permute-done.144 = f32[2,4,128,128]{3,2,1,0:T(8,128)S(1)} collective-permute-done((f32[2,4,128,128]{3,2,1,0:T(8,128)S(1)}, f32[2,4,128,128]{3,2,1,0:T(8,128)S(1)}, u32[]{:S(2)}, u32[]{:S(2)}) %collective-permute-start.144) | collective-permute-done | bytes 524320 | tf_op jit(solution)/shard_map/cond/branch_52_fun/ppermute | solution.py:16
  101.2 3.1 collective-permute-start.145
  104.3 10.7 %collective-permute-done.145 = f32[2,4,128,128]{3,2,1,0:T(8,128)S(1)} collective-permute-done((f32[2,4,128,128]{3,2,1,0:T(8,128)S(1)}, f32[2,4,128,128]{3,2,1,0:T(8,128)S(1)}, u32[]{:S(2)}, u32[]{:S(2)}) %collective-permute-start.145) | collective-permute-done | bytes 524320 | tf_op jit(solution)/shard_map/cond/branch_52_fun/ppermute | solution.py:16
  114.9 4.6 %collective-permute-start.146 = (f32[2,4,128,128]{3,2,1,0:T(8,128)S(1)}, f32[2,4,128,128]{3,2,1,0:T(8,128)}, u32[]{:S(2)}, u32[]{:S(2)}) collective-permute-start(f32[2,4,128,128]{3,2,1,0:T(8,128)S(1)} %collective-permute-done.145), channel_id=1, source_target_pairs={{0,256},{8,264},{16,272},{24,280},{32,288},{40,296},{48,304},{56,3... | collective-permute-start | bytes 1572872 | tf_op jit(solution)/shard_map/cond/branch_52_fun/ppermute | solution.py:16
  119.6 9.8 %collective-permute-done.146 = f32[2,4,128,128]{3,2,1,0:T(8,128)} collective-permute-done((f32[2,4,128,128]{3,2,1,0:T(8,128)S(1)}, f32[2,4,128,128]{3,2,1,0:T(8,128)}, u32[]{:S(2)}, u32[]{:S(2)}) %collective-permute-start.146) | collective-permute-done | bytes 524320 | tf_op jit(solution)/shard_map/cond/branch_52_fun/ppermute | solution.py:16
  129.4 1.8 slice_bitcast_fusion.1
  131.2 2.0 reshape.369
  133.1 2.0 reshape.367
  135.1 1.9 reshape.368
  140.2 1.5 select_select_fusion
  142.7 58.2 %while.15 = (s32[]{:T(128)}, f32[4,128,128]{2,1,0:T(8,128)S(1)}, f32[4,128,4,128]{1,3,2,0:T(8,128)}, f32[4,1,1]{0,2,1:T(1,128)}, s32[4]{0:T(128)}, /*index=5*/bf...) while((s32[]{:T(128)}, f32[4,128,128]{2,1,0:T(8,128)S(1)}, ...), condition=%wide.region_64.65_spmd, body=%wide.region_63.64_spmd.sunk | while | flops 151783680 | bytes 3321469 | solution.py:110
  142.7 1.2 dynamic_slice.69
  145.2 1.2 multiply_exponential_fusion.5
  146.4 1.3 multiply_exponential_fusion.4
  148.5 1.6 constant_dynamic-slice_fusion.8
  150.1 1.7 constant_dynamic-slice_fusion.9
  151.8 2.0 convolution_bitcast_fusion.3
  153.8 2.1 fusion.64
  155.9 1.3 convolution_add_fusion.2
  157.2 1.2 dynamic_slice.69
  159.7 1.2 multiply_exponential_fusion.5
  161.0 1.3 multiply_exponential_fusion.4
  163.0 1.6 constant_dynamic-slice_fusion.8
  164.6 1.7 constant_dynamic-slice_fusion.9
  166.3 2.0 convolution_bitcast_fusion.3
  168.4 2.1 fusion.64
  170.4 1.3 convolution_add_fusion.2
  174.3 1.2 multiply_exponential_fusion.5
  175.5 1.3 multiply_exponential_fusion.4
  177.6 1.6 constant_dynamic-slice_fusion.8
  179.2 1.7 constant_dynamic-slice_fusion.9
  180.9 2.0 convolution_bitcast_fusion.3
  183.0 2.0 fusion.64
  185.0 1.3 convolution_add_fusion.2
  186.3 1.2 dynamic_slice.69
  188.8 1.2 multiply_exponential_fusion.5
  190.1 1.3 multiply_exponential_fusion.4
  192.1 1.6 constant_dynamic-slice_fusion.8
  193.7 1.7 constant_dynamic-slice_fusion.9
  195.5 2.0 convolution_bitcast_fusion.3
  197.5 2.0 fusion.64
  199.5 1.3 convolution_add_fusion.2
  201.6 3.0 gather_fusion.1
  204.6 2.3 fusion.17
  207.6 1.2 copy.59
  209.0 2.0 fusion.21
  211.7 1.3 copy.57
  213.0 1.3 multiply_reduce_fusion
  214.4 2.5 copy.46
  217.7 4.8 %convolution_convert_fusion = bf16[512,3072]{1,0:T(8,128)(2,1)} fusion(bf16[512,3072]{1,0:T(8,128)(2,1)S(1)} %copy-done, f32[64,8,4,128]{3,2,1,0:T(4,128)S(1)} %bitcast.148, f32[64,8,4,128]{3,2,1,0:T(4,128)} %bitcast.149, pred[512]{0:T(512)(128)(4,1)S(1)} %iota_compare_fusion.2), kind=kOutput, calls=%fused_computation.37 | convolution fusion | flops 1612972032 | bytes 8389120 | tf_op jit(solution)/shard_map/dot_general | solution.py:119
  222.5 4.7 %copy.55 = bf16[512,3072]{0,1:T(8,128)(2,1)} copy(bf16[512,3072]{1,0:T(8,128)(2,1)} %convolution_convert_fusion) | data formatting | bytes 6291456
  227.1 25.5 %reduce-scatter.14.cloned.1.call-done = bf16[384,4]{1,0:T(8,128)(2,1)} async-done(((bf16[3072,4]{1,0:T(8,128)(2,1)}), bf16[384,4]{1,0:T(8,128)(2,1)}) %reduce-scatter.14.cloned.1.call-update) | async-done | bytes 3088
  253.7 40.1 %reduce-scatter.12.cloned.1.call-done = bf16[384,4]{1,0:T(8,128)(2,1)} async-done(((bf16[3072,4]{1,0:T(8,128)(2,1)}), bf16[384,4]{1,0:T(8,128)(2,1)}) %reduce-scatter.12.cloned.1.call-update) | async-done | bytes 3088
  295.3 43.3 %reduce-scatter.10.cloned.1.call-done = bf16[384,512]{1,0:T(8,128)(2,1)} async-done(((bf16[3072,512]{1,0:T(8,128)(2,1)}), bf16[384,512]{1,0:T(8,128)(2,1)}) %reduce-scatter.10.cloned.1.call-update) | async-done | bytes 393232
  338.6 1.9 copy.56
  (80 shorter events, 26.0 us)
Async XLA Ops:
  7.2 199.9 %copy-start = (bf16[512,3072]{1,0:T(8,128)(2,1)S(1)}, bf16[512,3072]{1,0:T(8,128)(2,1)}, u32[]{:S(2)}) copy-start(bf16[512,3072]{1,0:T(8,128)(2,1)} %param.94) | copy-start | bytes 9437188
  7.2 245.5 %reduce-scatter.14.cloned.1.call-start = ((), (), s32[]{:S(2)}) async-start(), calls=%async_computation.5 | async-start | bytes 884736
  31.4 11.4 %collective-permute-start.143 = (f32[2,4,128,128]{3,2,1,0:T(8,128)S(1)}, f32[2,4,128,128]{3,2,1,0:T(8,128)S(1)}, u32[]{:S(2)}, u32[]{:S(2)}) collective-permute-start(f32[2,4,128,128]{3,2,1,0:T(8,128)S(1)} %param.52), channel_id=1, source_target_pairs={{0,8},{8,0},{16,24},{24,16},{32,40},{40,32},{48,56},{56,48},{64,72... | collective-permute-start | bytes 1572872 | tf_op jit(solution)/shard_map/cond/branch_52_fun/ppermute | solution.py:16
  42.8 58.3 %collective-permute-start.144 = (f32[2,4,128,128]{3,2,1,0:T(8,128)S(1)}, f32[2,4,128,128]{3,2,1,0:T(8,128)S(1)}, u32[]{:S(2)}, u32[]{:S(2)}) collective-permute-start(f32[2,4,128,128]{3,2,1,0:T(8,128)S(1)} %collective-permute-done.143), channel_id=1, source_target_pairs={{0,32},{8,40},{16,48},{24,56},{32,0},{40,8},{48,16},{56,24},{64,96... | collective-permute-start | bytes 1572872 | tf_op jit(solution)/shard_map/cond/branch_52_fun/ppermute | solution.py:16
  101.2 13.8 %collective-permute-start.145 = (f32[2,4,128,128]{3,2,1,0:T(8,128)S(1)}, f32[2,4,128,128]{3,2,1,0:T(8,128)S(1)}, u32[]{:S(2)}, u32[]{:S(2)}) collective-permute-start(f32[2,4,128,128]{3,2,1,0:T(8,128)S(1)} %collective-permute-done.144), channel_id=1, source_target_pairs={{0,128},{8,136},{16,144},{24,152},{32,160},{40,168},{48,176},{56,1... | collective-permute-start | bytes 1572872 | tf_op jit(solution)/shard_map/cond/branch_52_fun/ppermute | solution.py:16
  114.9 14.5 %collective-permute-start.146 = (f32[2,4,128,128]{3,2,1,0:T(8,128)S(1)}, f32[2,4,128,128]{3,2,1,0:T(8,128)}, u32[]{:S(2)}, u32[]{:S(2)}) collective-permute-start(f32[2,4,128,128]{3,2,1,0:T(8,128)S(1)} %collective-permute-done.145), channel_id=1, source_target_pairs={{0,256},{8,264},{16,272},{24,280},{32,288},{40,296},{48,304},{56,3... | collective-permute-start | bytes 1572872 | tf_op jit(solution)/shard_map/cond/branch_52_fun/ppermute | solution.py:16
  141.7 1.0 copy-start.1
  204.6 4.3 %copy-start.2 = (bf16[1,4,512]{2,1,0:T(4,128)(2,1)S(1)}, bf16[1,4,512]{2,1,0:T(4,128)(2,1)}, u32[]{:S(2)}) copy-start(bf16[1,4,512]{2,1,0:T(4,128)(2,1)} %get-tuple-element.330) | copy-start | bytes 12292
  204.6 4.4 %copy-start.3 = (f32[4,4,128]{2,1,0:T(4,128)S(1)}, f32[4,4,128]{2,1,0:T(4,128)}, u32[]{:S(2)}) copy-start(f32[4,4,128]{2,1,0:T(4,128)} %reshape.377) | copy-start | bytes 24580
  204.6 4.4 %copy-start.4 = (f32[4,4,128]{2,1,0:T(4,128)S(1)}, f32[4,4,128]{2,1,0:T(4,128)}, u32[]{:S(2)}) copy-start(f32[4,4,128]{2,1,0:T(4,128)} %reshape.378) | copy-start | bytes 24580
  204.6 4.4 %copy-start.5 = (f32[4]{0:T(128)S(1)}, f32[4]{0:T(128)}, u32[]{:S(2)}) copy-start(f32[4]{0:T(128)} %get-tuple-element.341) | copy-start | bytes 52
  204.6 4.4 %copy-start.6 = (pred[4]{0:T(512)(128)(4,1)S(1)}, pred[4]{0:T(512)(128)(4,1)}, u32[]{:S(2)}) copy-start(pred[4]{0:T(512)(128)(4,1)} %compare_and_fusion) | copy-start | bytes 16
  208.9 84.8 %reduce-scatter.12.cloned.1.call-start = ((), (), s32[]{:S(2)}) async-start(), calls=%async_computation.4 | async-start | bytes 884736
  213.0 125.7 %reduce-scatter.10.cloned.1.call-start = ((), (), s32[]{:S(2)}) async-start(), calls=%async_computation.3 | async-start | bytes 3538944
Sparse Core Ops, SparseCore 0:
  209.0 43.6 reduce-scatter.13
  255.7 37.9 reduce-scatter.11
  296.6 42.0 reduce-scatter.9
where the time goes:
time: 350 us; the launch traced here: 347 us
  waiting for transfers between devices  182 us (52%)
  local copies, waits for them, and re-layouts  56 us (16%)
  matrix products  31.8 us (9%)
  other arithmetic  28.8 us (8%)
  starting transfers between devices  25.5 us (7%)
  between operations  20.4 us (6%)
    unnamed x6, waiting for transfers between devices  109 us
    ppermute x4, waiting for transfers between devices, from_partner(): lax.ppermute(array, axis, [(i, i ^ 1 << apart) for i in range(lax.axis_si...  72.6 us
    ppermute x4, starting transfers between devices, from_partner(): lax.ppermute(array, axis, [(i, i ^ 1 << apart) for i in range(lax.axis_si...  25.4 us
    dynamic_slice x12, local copies, waits for them, and re-layouts, on_device(): lax.scan(partial(prefill_block, slopes=slopes), start_state, (shaped(q_pr...  18 us
    unnamed x20, local copies, waits for them, and re-layouts  12 us
    dot_general x4, matrix products, prefill_block(): jnp.einsum('hrc,chd->rhd', attn_weights, v_block, preferred_element_type=...  8.19 us
    dot_general x4, matrix products, prefill_block(): jnp.einsum('rhd,hde->rhe', q_block.astype(jnp.float32), memory, precision...  8.17 us
  transfers between devices with their start and end apart: 7, of which 7 were waited for; matrix products, arithmetic and copies ran while one was open for 6% of the time, Pallas kernels for 0%

commit v1 on v0

v1 whole, which is shorter than its diff:
```python
from functools import partial

import jax
import jax.numpy as jnp
from jax import lax
from jax.experimental import pallas as pl
from jax.experimental.pallas import tpu as pltpu
from jax.sharding import PartitionSpec as P

DK = 128
BLK = 128
EPS = 1e-06
PAD = 16
VMEM_LIMIT = 48 * 1024 * 1024
ORDER = (2, 1, 3, 0)


def params(axes=1):
    return pltpu.CompilerParams(
        dimension_semantics=("arbitrary",) * axes, vmem_limit_bytes=VMEM_LIMIT
    )


def dot(left, right, left_dim=1, right_dim=0):
    return lax.dot_general(
        left, right, (((left_dim,), (right_dim,)), ((), ())), preferred_element_type=jnp.float32
    )


def split_dot(left, right):
    high = right.astype(jnp.bfloat16)
    low = (right - high.astype(jnp.float32)).astype(jnp.bfloat16)
    return dot(left, high) + dot(left, low)


def pack_kernel(own_ref, ids_ref, states_ref, out_ref):
    out_ref[...] = states_ref[...].astype(jnp.bfloat16)


def pack(own, send_ids, states):
    _, heads, rows, cols = states.shape
    count = send_ids.shape[1]
    block = (1, heads, rows, cols)
    return pl.pallas_call(
        pack_kernel,
        out_shape=jax.ShapeDtypeStruct((count, heads, rows, cols), jnp.bfloat16),
        grid_spec=pltpu.PrefetchScalarGridSpec(
            num_scalar_prefetch=2,
            grid=(count,),
            in_specs=[pl.BlockSpec(block, lambda j, own, ids: (ids[own[0], j], 0, 0, 0))],
            out_specs=pl.BlockSpec(block, lambda j, own, ids: (j, 0, 0, 0)),
        ),
        compiler_params=params(),
        name="pack",
    )(own, send_ids, states)


def intra_kernel(len_ref, slopes_ref, q_ref, k_ref, v_ref, att_ref, mem_ref):
    slope = slopes_ref[pl.program_id(0)]
    length = len_ref[0]
    rows = lax.broadcasted_iota(jnp.int32, (BLK, BLK), 0)
    cols = lax.broadcasted_iota(jnp.int32, (BLK, BLK), 1)
    damping = jnp.exp(-slope * jnp.maximum(rows - cols, 0).astype(jnp.float32))
    leading = jnp.exp(-slope * (rows + 1).astype(jnp.float32))
    mem_ref[...] = jnp.zeros_like(mem_ref)

    def step(block, carry):
        count = jnp.clip(length - block * BLK, 0, BLK)
        here = pl.ds(pl.multiple_of(block * BLK, BLK), BLK)
        q_block, k_block, v_block = q_ref[here, :], k_ref[here, :], v_ref[here, :]
        memory = mem_ref[0]
        scores = dot(q_block, k_block, 1, 1)
        kept = (cols <= rows) & (cols < count)
        probs = jnp.where(kept, scores * damping, 0.0).astype(jnp.bfloat16)
        att_ref[here, :] = dot(probs, v_block) + leading * split_dot(q_block, memory)
        behind = jnp.maximum(count - 1 - rows, 0).astype(jnp.float32)
        trailing = jnp.where(rows < count, jnp.exp(-slope * behind), 0.0)
        weighted = (k_block.astype(jnp.float32) * trailing).astype(jnp.bfloat16)
        fade = jnp.exp(jnp.full((1, DK), -slope * count.astype(jnp.float32)))
        mem_ref[0] = fade * memory + dot(weighted, v_block, 0, 0)
        return carry

    lax.fori_loop(0, q_ref.shape[0] // BLK, step, 0)


def intra(prompt_len, slopes, q_prefill, k_prefill, v_prefill):
    tokens, width = q_prefill.shape
    heads = width // DK
    column = pl.BlockSpec((tokens, DK), lambda h: (0, h))
    scalar = pl.BlockSpec(memory_space=pltpu.SMEM)
    return pl.pallas_call(
        intra_kernel,
        out_shape=(
            jax.ShapeDtypeStruct((tokens, width), jnp.float32),
            jax.ShapeDtypeStruct((heads, DK, DK), jnp.float32),
        ),
        grid=(heads,),
        in_specs=[scalar, scalar, column, column, column],
        out_specs=(column, pl.BlockSpec((1, DK, DK), lambda h: (h, 0, 0))),
        compiler_params=params(),
        cost_estimate=pl.CostEstimate(
            flops=10 * tokens * BLK * width, bytes_accessed=5 * tokens * width * 2, transcendentals=0
        ),
        name="intra",
    )(prompt_len, slopes, q_prefill, k_prefill, v_prefill)


def head_norm(inputs):
    return inputs * lax.rsqrt(jnp.mean(inputs * inputs, axis=-1, keepdims=True) + EPS)


def serve_kernel(
    place_ref, partner_ref, ids_ref, count_ref, slot_ref, len_ref, decode_ref, slopes_ref,
    states_ref, payload_ref, att_ref, mem_ref, q_ref, qd_ref, kd_ref, vd_ref, w_ref,
    normed_ref, out_ref, held_ref, served_ref,
):
    step = pl.program_id(0)
    heads = held_ref.shape[0]
    tokens = q_ref.shape[0]
    own = place_ref[0]
    mate = partner_ref[own]
    prefill_slot = slot_ref[0]
    length = len_ref[0]
    entries = ids_ref.shape[1]

    def moved(slot):
        memory = states_ref[slot, 0]
        for entry in range(entries):
            leaves = (ids_ref[own, entry] == slot) & (entry < count_ref[own])
            memory = jnp.where(leaves, 0.0, memory)
        for entry in range(entries):
            lands = (ids_ref[mate, entry] == slot) & (entry < count_ref[mate])
            memory = jnp.where(lands, payload_ref[entry, 0].astype(jnp.float32), memory)
        return memory

    @pl.when(step < heads)
    def _():
        slope = slopes_ref[step]
        start = moved(prefill_slot)
        rows = lax.broadcasted_iota(jnp.int32, (tokens, DK), 0)
        leading = jnp.exp(-slope * (rows + 1).astype(jnp.float32))
        attended = att_ref[...] + leading * split_dot(q_ref[...], start)
        normed = jnp.where(rows < length, head_norm(attended), 0.0).astype(jnp.bfloat16)
        held_ref[step, :tokens, :] = normed
        normed_ref[:tokens, :] = normed

        fade = jnp.exp(jnp.full((1, DK), -slope * length.astype(jnp.float32)))
        keep = jnp.exp(jnp.full((1, DK), -slope))
        final = fade * start + mem_ref[0]
        slots = decode_ref.shape[1]
        first_rows, second_rows = [], []
        q_all = qd_ref[...].astype(jnp.float32)
        k_all = kd_ref[...].astype(jnp.float32)
        v_all = vd_ref[...].astype(jnp.float32)
        for row in range(slots):
            slot = decode_ref[0, row]
            memory = jnp.where(slot == prefill_slot, final, moved(slot))
            query = qd_ref[:, row, :]
            seen = split_dot(jnp.concatenate([query] * 8, axis=0), memory)
            q_now, k_now, v_now = q_all[:, row], k_all[:, row], v_all[:, row]
            pair = lambda e, f: jnp.sum(q_now[e : e + 1] * k_now[f : f + 1], axis=-1, keepdims=True)
            first = keep * seen[0:1] + pair(0, 0) * v_now[0:1]
            second = (
                keep * (keep * seen[1:2] + pair(1, 0) * v_now[0:1]) + pair(1, 1) * v_now[1:2]
            )
            first_rows.append(first)
            second_rows.append(second)
        decoded = head_norm(jnp.concatenate(first_rows + second_rows, axis=0))
        padding = jnp.zeros((PAD - decoded.shape[0], DK), jnp.float32)
        decoded = jnp.concatenate([decoded, padding], axis=0).astype(jnp.bfloat16)
        held_ref[step, tokens:, :] = decoded
        normed_ref[tokens:, :] = decoded

    @pl.when(step >= heads)
    def _():
        total = dot(held_ref[0], w_ref[:DK, :])
        for head in range(1, heads):
            total += dot(held_ref[head], w_ref[head * DK : (head + 1) * DK, :])
        out_ref[0] = total.astype(jnp.bfloat16)


def far_chip(place, step):
    return lax.rem(place[1] // 2 + jnp.where(step == 0, ORDER[0], jnp.where(step == 1, ORDER[1], jnp.where(step == 2, ORDER[2], ORDER[3]))), 4)


def serve(place, scalars, states, payload, attended, memory, q_prefill, decode, w_out):
    slots, heads = states.shape[:2]
    tokens, width = q_prefill.shape
    cols = w_out.shape[1] // 8
    steps = decode[0].shape[0]
    rows = tokens + PAD
    at = lambda s: jnp.minimum(s, heads - 1)
    dest = lambda s: jnp.maximum(s - heads, 0)
    column = pl.BlockSpec((tokens, DK), lambda s, *_: (0, at(s)))
    row = pl.BlockSpec((steps, slots, DK), lambda s, *_: (0, 0, at(s)))
    w_block = pl.BlockSpec(
        (width, cols),
        lambda s, place, *_: (0, 2 * far_chip(place, dest(s)) + 1 - lax.rem(place[1], 2)),
    )
    return pl.pallas_call(
        serve_kernel,
        out_shape=(
            jax.ShapeDtypeStruct((rows, width), jnp.bfloat16),
            jax.ShapeDtypeStruct((4, rows, cols), jnp.bfloat16),
        ),
        grid_spec=pltpu.PrefetchScalarGridSpec(
            num_scalar_prefetch=8,
            grid=(heads + 4,),
            in_specs=[
                pl.BlockSpec((slots, 1, DK, DK), lambda s, *_: (0, at(s), 0, 0)),
                pl.BlockSpec((payload.shape[0], 1, DK, DK), lambda s, *_: (0, at(s), 0, 0)),
                column,
                pl.BlockSpec((1, DK, DK), lambda s, *_: (at(s), 0, 0)),
                column,
                row,
                row,
                row,
                w_block,
            ],
            out_specs=(
                pl.BlockSpec((rows, DK), lambda s, *_: (0, at(s))),
                pl.BlockSpec((1, rows, cols), lambda s, *_: (dest(s), 0, 0)),
            ),
            scratch_shapes=[
                pltpu.VMEM((heads, rows, DK), jnp.bfloat16),
                pltpu.VMEM((8, DK), jnp.float32),
            ],
        ),
        compiler_params=params(),
        name="serve",
    )(place, *scalars, states, payload, attended, memory, q_prefill, *decode, w_out)


def join_kernel(place_ref, normed_ref, w_ref, other_ref, *out_refs):
    step = pl.program_id(0)
    total = dot(normed_ref[...], w_ref[...]) + other_ref[0].astype(jnp.float32)
    rounded = total.astype(jnp.bfloat16)
    for index, out_ref in enumerate(out_refs):

        @pl.when(step == index)
        def _():
            out_ref[...] = rounded


def join(place, normed, w_out, other):
    rows, width = normed.shape
    cols = w_out.shape[1] // 8
    return pl.pallas_call(
        join_kernel,
        out_shape=(jax.ShapeDtypeStruct((rows, cols), jnp.bfloat16),) * 4,
        grid_spec=pltpu.PrefetchScalarGridSpec(
            num_scalar_prefetch=1,
            grid=(4,),
            in_specs=[
                pl.BlockSpec((rows, width), lambda s, *_: (0, 0)),
                pl.BlockSpec(
                    (width, cols),
                    lambda s, place: (0, 2 * far_chip(place, s) + lax.rem(place[1], 2)),
                ),
                pl.BlockSpec((1, rows, cols), lambda s, *_: (s, 0, 0)),
            ],
            out_specs=(pl.BlockSpec((rows, cols), lambda s, *_: (0, 0)),) * 4,
        ),
        compiler_params=params(),
        name="join",
    )(place, normed, w_out, other)


def finish_kernel(a_ref, b_ref, c_ref, d_ref, prefill_ref, decode_ref):
    total = a_ref[...].astype(jnp.float32) + b_ref[...].astype(jnp.float32)
    total += c_ref[...].astype(jnp.float32)
    total += d_ref[...].astype(jnp.float32)
    rounded = total.astype(jnp.bfloat16)
    tokens = prefill_ref.shape[0]
    prefill_ref[...] = rounded[:tokens]
    steps, slots, _ = decode_ref.shape
    for step in range(steps):
        first = tokens + step * slots
        decode_ref[step] = total[first : first + slots].astype(jnp.bfloat16)


def finish(parts, tokens, steps, slots):
    cols = parts[0].shape[1]
    return pl.pallas_call(
        finish_kernel,
        out_shape=(
            jax.ShapeDtypeStruct((tokens, cols), jnp.bfloat16),
            jax.ShapeDtypeStruct((steps, slots, cols), jnp.bfloat16),
        ),
        compiler_params=params(0),
        name="finish",
    )(*parts)


def exchange(array, pattern):
    size = lax.axis_size("replica")
    return lax.ppermute(array, "replica", [(i, i ^ pattern) for i in range(size)])


def on_device(
    states,
    partner,
    send_ids,
    send_count,
    prefill_slot,
    prompt_len,
    decode_slots,
    q_prefill,
    k_prefill,
    v_prefill,
    q_decode,
    k_decode,
    v_decode,
    slopes,
    w_out,
):
    size = lax.axis_size("replica")
    own = lax.axis_index("replica")
    head = lax.axis_index("head")
    place = jnp.stack([own, head]).astype(jnp.int32)
    payload = pack(place, send_ids, states)

    half, across = size // 2, size // 4 * 3

    def branch(pattern, payload, *prefill):
        moving = payload
        if pattern >= half:
            moving = exchange(moving, across)
            pattern ^= across
        if pattern:
            moving = exchange(moving, pattern)
        return moving, *intra(*prefill)

    payload, attended, memory = lax.switch(
        jnp.clip(partner[0] - 1, 0, size - 2),
        [partial(branch, pattern) for pattern in range(1, size)],
        payload,
        prompt_len,
        slopes,
        q_prefill,
        k_prefill,
        v_prefill,
    )
    scalars = (partner, send_ids, send_count, prefill_slot, prompt_len, decode_slots, slopes)
    normed, other = serve(
        place, scalars, states, payload, attended, memory, q_prefill,
        (q_decode, k_decode, v_decode), w_out,
    )
    devices = lax.axis_size("head")
    other = lax.ppermute(other, "head", [(i, i ^ 1) for i in range(devices)])
    parts = join(place, normed, w_out, other)
    arrived = [
        lax.ppermute(part, "head", [(i, (i + 2 * away) % devices) for i in range(devices)])
        if away
        else part
        for away, part in zip(ORDER, parts, strict=True)
    ]
    steps, slots = q_decode.shape[:2]
    return finish(arrived, q_prefill.shape[0], steps, slots)


def solution(mesh):
    return jax.shard_map(
        on_device,
        mesh=mesh,
        in_specs=(
            P("replica", "head", None, None),
            P(),
            P(),
            P(),
            P("replica"),
            P("replica"),
            P("replica", None),
            P("replica", "head"),
            P("replica", "head"),
            P("replica", "head"),
            P(None, "replica", "head"),
            P(None, "replica", "head"),
            P(None, "replica", "head"),
            P("head"),
            P("head", None),
        ),
        out_specs=(P("replica", "head"), P(None, "replica", "head")),
        check_vma=False,
    )
```

time: 350 us -> 95.9 us (0.27)
  waiting for transfers between devices: 182 us -> 34 us
  local copies, waits for them, and re-layouts: 56 us -> 2.04 us
  matrix products: 31.8 us -> 0 us
  other arithmetic: 28.8 us -> 0.07 us
  Pallas kernels: 0 us -> 21.6 us
  between operations: 20.4 us -> 2.76 us
  starting transfers between devices: 25.5 us -> 33.9 us
    unnamed x6 -> x0, waiting for transfers between devices: 109 us -> none
    ppermute x4 -> x6, waiting for transfers between devices: 72.6 us -> 34 us  [the longest x2 18.9 us: exchange(): lax.ppermute(array, 'replica', [(i, i ^ pattern) for i in range(size)])]
    dot_general x17 -> x0, matrix products: 31.8 us -> none  [the longest x4 8.19 us: prefill_block(): jnp.einsum('hrc,chd->rhd', attn_weights, v_block, preferred_element_type=...]
    dynamic_slice x15 -> x0, local copies, waits for them, and re-layouts: 21.7 us -> none  [the longest x12 18 us: on_device(): lax.scan(partial(prefill_block, slopes=slopes), start_state, (shaped(q_pr...]
    pallas_call x0 -> x5, Pallas kernels: none -> 21.6 us  [the longest x1 8.55 us: serve(): pl.pallas_call(serve_kernel, out_shape=(jax.ShapeDtypeStruct((rows, width...]
    exp x9 -> x0, other arithmetic: 11.5 us -> none  [the longest x4 5.36 us: prefill_block(): leading = jnp.exp(-slopes[None, :] * (places[:, None] + 1.0))]
    unnamed x20 -> x17, local copies, waits for them, and re-layouts: 12 us -> 2.04 us
    ppermute x4 -> x6, starting transfers between devices: 25.4 us -> 33.9 us  [the longest x2 19.2 us: exchange(): lax.ppermute(array, 'replica', [(i, i ^ pattern) for i in range(size)])]
  transfers between devices with their start and end apart: 7 -> 6, of which waited for: 7 -> 5; matrix products, arithmetic and copies ran while one was open for 6% -> 0% of each run, Pallas kernels for 0% -> 7%
where the time goes in v1:
time: 95.9 us; the launch traced here: 95.1 us
  waiting for transfers between devices  34 us (35%)
  starting transfers between devices  33.9 us (35%)
  Pallas kernels  21.6 us (23%)
  between operations  2.76 us (3%)
  local copies, waits for them, and re-layouts  2.04 us (2%)
    ppermute x2, starting transfers between devices, exchange(): lax.ppermute(array, 'replica', [(i, i ^ pattern) for i in range(size)])  19.2 us
    ppermute x2, waiting for transfers between devices, exchange(): lax.ppermute(array, 'replica', [(i, i ^ pattern) for i in range(size)])  18.9 us
    ppermute x3, waiting for transfers between devices, on_device(): lax.ppermute(part, 'head', [(i, (i + 2 * away) % devices) for i in range(...  12 us
    ppermute x3, starting transfers between devices, on_device(): lax.ppermute(part, 'head', [(i, (i + 2 * away) % devices) for i in range(...  11.3 us
    pallas_call x1, Pallas kernels, serve(): pl.pallas_call(serve_kernel, out_shape=(jax.ShapeDtypeStruct((rows, width...  8.55 us
    pallas_call x1, Pallas kernels, intra(): pl.pallas_call(intra_kernel, out_shape=(jax.ShapeDtypeStruct((tokens, wid...  6.75 us
    pallas_call x1, Pallas kernels, join(): pl.pallas_call(join_kernel, out_shape=(jax.ShapeDtypeStruct((rows, cols),...  4.16 us
    ppermute x1, starting transfers between devices, on_device(): other = lax.ppermute(other, 'head', [(i, i ^ 1) for i in range(devices)])  3.38 us
  transfers between devices with their start and end apart: 6, of which 5 were waited for; matrix products, arithmetic and copies ran while one was open for 0% of the time, Pallas kernels for 7%

profile of v1, /device:TPU:1, one launch (start us, length us, event | category | flops | bytes accessed | tf_op | source)
XLA Modules:
  0.0 95.1 jit_solution(10172258805599417768)
XLA Ops:
  2.6 0.8 copy.18.ids_ref
  3.3 0.1 pad_add_fusion.own_ref.place_ref
  3.4 0.0 copy-start
  3.4 1.2 %copy-done = f32[4,4,128,128]{3,2,1,0:T(8,128)S(1)} copy-done((f32[4,4,128,128]{3,2,1,0:T(8,128)S(1)}, f32[4,4,128,128]{3,2,1,0:T(8,128)}, u32[]{:S(2)}) %copy-start) | copy-done | bytes 1048600
  4.7 1.2 %pack.1 = bf16[2,4,128,128]{3,2,1,0:T(8,128)(2,1)S(1)} custom-call(s32[2]{0:T(128)S(1)} %pad_add_fusion.own_ref.place_ref, s32[64,2]{1,0:T(8,128)S(1)} %copy.18.ids_ref, f32[4,4,128,128]{3,2,1,0:T(8,128)S(1)} %copy-done), custom_call_target="tpu_custom_call" | custom-call | tf_op jit(solution)/shard_map/pack/pallas_call | solution.py:44
  5.8 0.0 copy-start.1
  5.8 0.0 copy-start.2
  5.8 0.0 copy-start.3
  5.9 0.0 copy-start.4
  5.9 0.0 copy-start.5
  5.9 0.0 copy-start.6
  5.9 0.0 copy-start.7
  5.9 45.6 %conditional.1 = (bf16[2,4,128,128]{3,2,1,0:T(8,128)(2,1)}, f32[512,512]{1,0:T(8,128)S(1)}, f32[4,128,128]{2,1,0:T(8,128)S(1)}) conditional(s32[]{:T(128)} %bitcast.2, (bf16[2,4,128,128]{3,2,1,0:T(8,128)(2,1)S(1)}, s32[1]{0:T(128)}, f32[4]{0:T(128)}, bf16[512,512]{1,0:T(8,128)(2,1)}, bf16[512,512]{1,0:T(8,128)(2,1)}, ...), branch_computations={%region_0.1_spmd, %region_1.2_spmd, %region_2.3_spmd, %region_3.4_... | conditional | flops 335544320 | bytes 4718696 | solution.py:334
  6.2 5.3 %collective-permute-start.57 = (bf16[2,4,128,128]{3,2,1,0:T(8,128)(2,1)S(1)}, bf16[2,4,128,128]{3,2,1,0:T(8,128)(2,1)S(1)}, u32[]{:S(2)}, u32[]{:S(2)}) collective-permute-start(bf16[2,4,128,128]{3,2,1,0:T(8,128)(2,1)S(1)} %get-tuple-element.1108), channel_id=1, source_target_pairs={{0,384},{8,392},{16,400},{24,408},{32,416},{40,424},{48,432},{56,4... | collective-permute-start | bytes 786440 | tf_op jit(solution)/shard_map/cond/branch_44_fun/ppermute | solution.py:297
  11.6 3.7 %collective-permute-done.57 = bf16[2,4,128,128]{3,2,1,0:T(8,128)(2,1)S(1)} collective-permute-done((bf16[2,4,128,128]{3,2,1,0:T(8,128)(2,1)S(1)}, bf16[2,4,128,128]{3,2,1,0:T(8,128)(2,1)S(1)}, u32[]{:S(2)}, u32[]{:S(2)}) %collective-permute-start.57) | collective-permute-done | bytes 262176 | tf_op jit(solution)/shard_map/cond/branch_44_fun/ppermute | solution.py:297
  15.3 13.9 %collective-permute-start.58 = (bf16[2,4,128,128]{3,2,1,0:T(8,128)(2,1)S(1)}, bf16[2,4,128,128]{3,2,1,0:T(8,128)(2,1)}, u32[]{:S(2)}, u32[]{:S(2)}) collective-permute-start(bf16[2,4,128,128]{3,2,1,0:T(8,128)(2,1)S(1)} %collective-permute-done.57), channel_id=1, source_target_pairs={{0,232},{8,224},{16,248},{24,240},{32,200},{40,192},{48,216},{56,2... | collective-permute-start | bytes 786440 | tf_op jit(solution)/shard_map/cond/branch_44_fun/ppermute | solution.py:297
  29.2 6.7 %intra.107 = (f32[512,512]{1,0:T(8,128)S(1)}, f32[4,128,128]{2,1,0:T(8,128)S(1)}) custom-call(s32[1]{0:T(128)} %get-tuple-element.1109.len_ref, f32[4]{0:T(128)} %get-tuple-element.1110.slopes_ref, bf16[512,512]{1,0:T(8,128)(2,1)} %get-tuple-element.1111.q_ref, bf16[512,512]{1,0:T(8,128)(2,1)} %get-tuple-element.1112.k_ref, ...), custom_call_target="tpu_custom_call" | custom-call | flops 335544320 | bytes 2621440 | tf_op jit(solution)/shard_map/cond/branch_44_fun/intra/pallas_call | solution.py:91
  35.9 15.1 %collective-permute-done.58 = bf16[2,4,128,128]{3,2,1,0:T(8,128)(2,1)} collective-permute-done((bf16[2,4,128,128]{3,2,1,0:T(8,128)(2,1)S(1)}, bf16[2,4,128,128]{3,2,1,0:T(8,128)(2,1)}, u32[]{:S(2)}, u32[]{:S(2)}) %collective-permute-start.58) | collective-permute-done | bytes 262176 | tf_op jit(solution)/shard_map/cond/branch_44_fun/ppermute | solution.py:297
  51.5 0.0 copy-done.1
  51.5 0.0 copy-done.2
  51.5 0.0 copy-done.3
  51.5 0.0 copy-done.4
  51.6 0.0 copy-done.5
  51.6 0.0 copy-done.6
  51.6 0.0 copy-done.7
  51.6 8.6 %serve.1 = (bf16[528,512]{1,0:T(8,128)(2,1)S(1)}, bf16[4,528,384]{2,1,0:T(8,128)(2,1)S(1)}) custom-call(s32[2]{0:T(128)S(1)} %pad_add_fusion.own_ref.place_ref, s32[64]{0:T(128)S(1)} %copy-done.5, s32[64,2]{1,0:T(8,128)S(1)} %copy.18.ids_ref, s32[64]{0:T(128)S(1)} %copy-done.6, s32[1]{0:T(128)S(6)} %copy.208.slot_ref, s32[1]{0:T(128)S(6)} %copy.209.len_ref, ...), custom_call_target="tpu_custom_call" | custom-call | tf_op jit(solution)/shard_map/serve/pallas_call | solution.py:200
  60.1 3.4 %collective-permute-start.94 = (bf16[4,528,384]{2,1,0:T(8,128)(2,1)S(1)}, bf16[4,528,384]{2,1,0:T(8,128)(2,1)S(1)}, u32[]{:S(2)}, u32[]{:S(2)}) collective-permute-start(bf16[4,528,384]{2,1,0:T(8,128)(2,1)S(1)} %get-tuple-element.1275), channel_id=1, source_target_pairs={{0,1},{1,0},{2,3},{3,2},{4,5},{5,4},{6,7},{7,6},{8,9},{9,8},{10,11... | collective-permute-start | bytes 4866056 | tf_op jit(solution)/shard_map/ppermute | solution.py:350
  63.5 3.1 %collective-permute-done.94.other_ref = bf16[4,528,384]{2,1,0:T(8,128)(2,1)S(1)} collective-permute-done((bf16[4,528,384]{2,1,0:T(8,128)(2,1)S(1)}, bf16[4,528,384]{2,1,0:T(8,128)(2,1)S(1)}, u32[]{:S(2)}, u32[]{:S(2)}) %collective-permute-start.94) | collective-permute-done | bytes 1622048 | tf_op jit(solution)/shard_map/ppermute | solution.py:350
  66.6 4.2 %join.1 = (bf16[528,384]{1,0:T(8,128)(2,1)S(1)}, bf16[528,384]{1,0:T(8,128)(2,1)S(1)}, bf16[528,384]{1,0:T(8,128)(2,1)S(1)}, bf16[528,384]{1,0:T(8,128)(2,1)S(1)}) custom-call(s32[2]{0:T(128)S(1)} %pad_add_fusion.own_ref.place_ref, bf16[528,512]{1,0:T(8,128)(2,1)S(1)} %get-tuple-element.1274.normed_ref, bf16[512,3072]{1,0:T(8,128)(2,1)} %w_ref.3, ...), custom_call_target="tpu_custom_call" | custom-call | tf_op jit(solution)/shard_map/join/pallas_call | solution.py:248
  70.8 4.8 %collective-permute-start.95 = (bf16[528,384]{1,0:T(8,128)(2,1)S(1)}, bf16[528,384]{1,0:T(8,128)(2,1)S(1)}, u32[]{:S(2)}, u32[]{:S(2)}) collective-permute-start(bf16[528,384]{1,0:T(8,128)(2,1)S(1)} %get-tuple-element.1276), channel_id=1, source_target_pairs={{0,4},{1,5},{2,6},{3,7},{4,0},{5,1},{6,2},{7,3},{8,12},{9,13},{10,... | collective-permute-start | bytes 1216520 | tf_op jit(solution)/shard_map/ppermute | solution.py:353
  75.6 2.3 %collective-permute-start.96 = (bf16[528,384]{1,0:T(8,128)(2,1)S(1)}, bf16[528,384]{1,0:T(8,128)(2,1)S(1)}, u32[]{:S(2)}, u32[]{:S(2)}) collective-permute-start(bf16[528,384]{1,0:T(8,128)(2,1)S(1)} %get-tuple-element.1277), channel_id=1, source_target_pairs={{0,2},{1,3},{2,4},{3,5},{4,6},{5,7},{6,0},{7,1},{8,10},{9,11},{10,... | collective-permute-start | bytes 1216520 | tf_op jit(solution)/shard_map/ppermute | solution.py:353
  77.9 4.2 %collective-permute-start.97 = (bf16[528,384]{1,0:T(8,128)(2,1)S(1)}, bf16[528,384]{1,0:T(8,128)(2,1)S(1)}, u32[]{:S(2)}, u32[]{:S(2)}) collective-permute-start(bf16[528,384]{1,0:T(8,128)(2,1)S(1)} %get-tuple-element.1278), channel_id=1, source_target_pairs={{0,6},{1,7},{2,0},{3,1},{4,2},{5,3},{6,4},{7,5},{8,14},{9,15},{10,... | collective-permute-start | bytes 1216520 | tf_op jit(solution)/shard_map/ppermute | solution.py:353
  82.1 2.7 %collective-permute-done.95.a_ref = bf16[528,384]{1,0:T(8,128)(2,1)S(1)} collective-permute-done((bf16[528,384]{1,0:T(8,128)(2,1)S(1)}, bf16[528,384]{1,0:T(8,128)(2,1)S(1)}, u32[]{:S(2)}, u32[]{:S(2)}) %collective-permute-start.95) | collective-permute-done | bytes 405536 | tf_op jit(solution)/shard_map/ppermute | solution.py:353
  84.8 9.4 %collective-permute-done.96.b_ref = bf16[528,384]{1,0:T(8,128)(2,1)S(1)} collective-permute-done((bf16[528,384]{1,0:T(8,128)(2,1)S(1)}, bf16[528,384]{1,0:T(8,128)(2,1)S(1)}, u32[]{:S(2)}, u32[]{:S(2)}) %collective-permute-start.96) | collective-permute-done | bytes 405536 | tf_op jit(solution)/shard_map/ppermute | solution.py:353
  94.2 0.0 collective-permute-done.97.c_ref
  94.2 1.0 %finish.1 = (bf16[512,384]{1,0:T(8,128)(2,1)}, bf16[2,4,384]{2,1,0:T(4,128)(2,1)}) custom-call(bf16[528,384]{1,0:T(8,128)(2,1)S(1)} %collective-permute-done.95.a_ref, bf16[528,384]{1,0:T(8,128)(2,1)S(1)} %collective-permute-done.96.b_ref, bf16[528,384]{1,0:T(8,128)(2,1)S(1)} %collective-permute-done.97.c_ref, bf16[528,384]{1,0:T(8,128)(2,1)S(1)} %get-tuple-element.1279.d_ref), custom_call_target="tpu_custom_call" | custom-call | tf_op jit(solution)/shard_map/finish/pallas_call | solution.py:284
Async XLA Ops:
  3.4 1.2 %copy-start = (f32[4,4,128,128]{3,2,1,0:T(8,128)S(1)}, f32[4,4,128,128]{3,2,1,0:T(8,128)}, u32[]{:S(2)}) copy-start(f32[4,4,128,128]{3,2,1,0:T(8,128)} %states_ref.3) | copy-start | bytes 3145732
  5.8 45.7 %copy-start.1 = (f32[4,4,128,128]{3,2,1,0:T(8,128)S(1)}, f32[4,4,128,128]{3,2,1,0:T(8,128)}, u32[]{:S(2)}) copy-start(f32[4,4,128,128]{3,2,1,0:T(8,128)} %states_ref.3) | copy-start | bytes 3145732
  5.8 45.7 %copy-start.2 = (bf16[2,4,512]{2,1,0:T(4,128)(2,1)S(1)}, bf16[2,4,512]{2,1,0:T(4,128)(2,1)}, u32[]{:S(2)}) copy-start(bf16[2,4,512]{2,1,0:T(4,128)(2,1)} %qd_ref.1) | copy-start | bytes 24580
  5.8 45.7 %copy-start.3 = (bf16[2,4,512]{2,1,0:T(4,128)(2,1)S(1)}, bf16[2,4,512]{2,1,0:T(4,128)(2,1)}, u32[]{:S(2)}) copy-start(bf16[2,4,512]{2,1,0:T(4,128)(2,1)} %kd_ref.1) | copy-start | bytes 24580
  5.9 45.7 %copy-start.4 = (bf16[2,4,512]{2,1,0:T(4,128)(2,1)S(1)}, bf16[2,4,512]{2,1,0:T(4,128)(2,1)}, u32[]{:S(2)}) copy-start(bf16[2,4,512]{2,1,0:T(4,128)(2,1)} %vd_ref.1) | copy-start | bytes 24580
  5.9 45.7 %copy-start.5 = (s32[64]{0:T(128)S(1)}, s32[64]{0:T(128)}, u32[]{:S(2)}) copy-start(s32[64]{0:T(128)} %partner_ref.1) | copy-start | bytes 772
  5.9 45.7 %copy-start.6 = (s32[64]{0:T(128)S(1)}, s32[64]{0:T(128)}, u32[]{:S(2)}) copy-start(s32[64]{0:T(128)} %count_ref.1) | copy-start | bytes 772
  5.9 45.7 %copy-start.7 = (s32[1,4]{1,0:T(1,128)S(1)}, s32[1,4]{1,0:T(1,128)}, u32[]{:S(2)}) copy-start(s32[1,4]{1,0:T(1,128)} %decode_ref.1) | copy-start | bytes 52
  6.2 9.1 %collective-permute-start.57 = (bf16[2,4,128,128]{3,2,1,0:T(8,128)(2,1)S(1)}, bf16[2,4,128,128]{3,2,1,0:T(8,128)(2,1)S(1)}, u32[]{:S(2)}, u32[]{:S(2)}) collective-permute-start(bf16[2,4,128,128]{3,2,1,0:T(8,128)(2,1)S(1)} %get-tuple-element.1108), channel_id=1, source_target_pairs={{0,384},{8,392},{16,400},{24,408},{32,416},{40,424},{48,432},{56,4... | collective-permute-start | bytes 786440 | tf_op jit(solution)/shard_map/cond/branch_44_fun/ppermute | solution.py:297
  15.3 35.7 %collective-permute-start.58 = (bf16[2,4,128,128]{3,2,1,0:T(8,128)(2,1)S(1)}, bf16[2,4,128,128]{3,2,1,0:T(8,128)(2,1)}, u32[]{:S(2)}, u32[]{:S(2)}) collective-permute-start(bf16[2,4,128,128]{3,2,1,0:T(8,128)(2,1)S(1)} %collective-permute-done.57), channel_id=1, source_target_pairs={{0,232},{8,224},{16,248},{24,240},{32,200},{40,192},{48,216},{56,2... | collective-permute-start | bytes 786440 | tf_op jit(solution)/shard_map/cond/branch_44_fun/ppermute | solution.py:297
  60.1 6.5 %collective-permute-start.94 = (bf16[4,528,384]{2,1,0:T(8,128)(2,1)S(1)}, bf16[4,528,384]{2,1,0:T(8,128)(2,1)S(1)}, u32[]{:S(2)}, u32[]{:S(2)}) collective-permute-start(bf16[4,528,384]{2,1,0:T(8,128)(2,1)S(1)} %get-tuple-element.1275), channel_id=1, source_target_pairs={{0,1},{1,0},{2,3},{3,2},{4,5},{5,4},{6,7},{7,6},{8,9},{9,8},{10,11... | collective-permute-start | bytes 4866056 | tf_op jit(solution)/shard_map/ppermute | solution.py:350
  70.8 14.0 %collective-permute-start.95 = (bf16[528,384]{1,0:T(8,128)(2,1)S(1)}, bf16[528,384]{1,0:T(8,128)(2,1)S(1)}, u32[]{:S(2)}, u32[]{:S(2)}) collective-permute-start(bf16[528,384]{1,0:T(8,128)(2,1)S(1)} %get-tuple-element.1276), channel_id=1, source_target_pairs={{0,4},{1,5},{2,6},{3,7},{4,0},{5,1},{6,2},{7,3},{8,12},{9,13},{10,... | collective-permute-start | bytes 1216520 | tf_op jit(solution)/shard_map/ppermute | solution.py:353
  75.6 18.6 %collective-permute-start.96 = (bf16[528,384]{1,0:T(8,128)(2,1)S(1)}, bf16[528,384]{1,0:T(8,128)(2,1)S(1)}, u32[]{:S(2)}, u32[]{:S(2)}) collective-permute-start(bf16[528,384]{1,0:T(8,128)(2,1)S(1)} %get-tuple-element.1277), channel_id=1, source_target_pairs={{0,2},{1,3},{2,4},{3,5},{4,6},{5,7},{6,0},{7,1},{8,10},{9,11},{10,... | collective-permute-start | bytes 1216520 | tf_op jit(solution)/shard_map/ppermute | solution.py:353
  77.9 16.2 %collective-permute-start.97 = (bf16[528,384]{1,0:T(8,128)(2,1)S(1)}, bf16[528,384]{1,0:T(8,128)(2,1)S(1)}, u32[]{:S(2)}, u32[]{:S(2)}) collective-permute-start(bf16[528,384]{1,0:T(8,128)(2,1)S(1)} %get-tuple-element.1278), channel_id=1, source_target_pairs={{0,6},{1,7},{2,0},{3,1},{4,2},{5,3},{6,4},{7,5},{8,14},{9,15},{10,... | collective-permute-start | bytes 1216520 | tf_op jit(solution)/shard_map/ppermute | solution.py:353
